TPU v7x, 256 devices: a whole 4x4x8 slice. The times are simulated.
256 devices in a mesh: section: 4 (over x_lo, core), ctx: 16 (over z, x_hi), tp: 4 (over y).
Axes of the slice: x: 4 (x_hi: 2, x_lo: 2; x = x_hi * 2 + x_lo), y: 4, z: 8, core: 2. Of those that a mesh axis runs over, the one named last changes fastest.
Arguments:
- in_weights: bfloat16 [4, 3, 4096, 4096], P('section', None, 'ctx', 'tp'), may hold values from -0.09375 to 0.09375
- short_taps: float32 [4, 3, 7, 4096], P('section', None, None, 'tp'), may hold values from -2 to 2
- long_taps: float32 [4, 128, 4096], P('section', None, 'tp'), may hold values from -0.5 to 0.5
- first_saved: bfloat16 [4, 3, 4096, 4096], P('section', None, 'ctx', 'tp'), may hold values from -6 to 6
- second_saved: bfloat16 [4, 3, 4096, 4096], P('section', None, 'ctx', 'tp'), may hold values from -6 to 6
- first_cotangent: bfloat16 [4, 4096, 4096], P('section', 'ctx', 'tp'), may hold values from -6 to 6
- last_cotangent: bfloat16 [4096, 4096], P('ctx', 'tp'), may hold values from -6 to 6
Outputs:
- first_sent: bfloat16 [4, 4096, 4096], P('section', 'ctx', 'tp')
- second_sent: bfloat16 [4, 4096, 4096], P('section', 'ctx', 'tp')
All inputs are finite; a program needn't handle non-finite values.
Results may differ from a plain program's by a relative error of at most 0.025.
Values may be sent and summed in bfloat16 or wider, within the bound.
A program may use at most 128 MiB of HBM per device.

v0:
```python
import functools

import numpy as np
import jax
import jax.numpy as jnp
from jax import lax
from jax.experimental import pallas as pl
from jax.experimental.pallas import tpu as pltpu
from jax.sharding import PartitionSpec as P

MESH = pl.DeviceIdType.MESH
N = 256
HALF = 128
BEFORE = 144
AFTER = 160
GROUP = 512
ROWS = BEFORE + GROUP + AFTER
REACH = GROUP + AFTER
KEPT = GROUP + 16
CHUNK = 256
TILE = 32
f32 = jnp.float32
bf16 = jnp.bfloat16


def shifted_dft():
    k = np.arange(HALF)[:, None] + 0.5
    n = np.arange(N)[None, :]
    angle = 2.0 * np.pi * k * n / N
    forward = np.concatenate([np.cos(angle), -np.sin(angle)], axis=0)
    return forward.astype(np.float32), (forward.T * (2.0 / N)).astype(np.float32)


FORWARD, INVERSE = shifted_dft()


def dot(a, b):
    return jnp.dot(a, b, preferred_element_type=f32)


def filtered(forward, inverse, signal, real, imag):
    spectrum = dot(forward, signal)
    a, b = spectrum[:HALF], spectrum[HALF:]
    mixed = jnp.concatenate([a * real - b * imag, a * imag + b * real], axis=0).astype(bf16)
    return dot(inverse, mixed)


def kernel(
    w_ref, short_ref, long_ref, u1_ref, u2_ref, g1_ref, gl_ref, fwd_ref, inv_ref, fwd32_ref,
    out1_ref, out2_ref,
    wb, ue, ge, p0, p1, p2, mx, di, pb, rb, sb, resp, pr, dm, df,
    ring_s, ring_r, x_s, x_r, loc, halo_s, halo_r, tp_s, tp_r, main_s, main_r, edge_s, edge_r,
    fin_s, fin_r,
):
    s = lax.axis_index("section")
    c = lax.axis_index("ctx")
    k = lax.axis_index("tp")
    z, h = c // 2, c % 2
    up, down = (z + 1) % 8, (z + 7) % 8
    partner = 2 * z + 1 - h
    last = s == 3

    def remote(src, dst, send, recv, device):
        return pltpu.make_async_remote_copy(
            src_ref=src, dst_ref=dst, send_sem=send, recv_sem=recv,
            device_id=device, device_id_type=MESH,
        )

    barrier = pltpu.get_barrier_semaphore()

    def greet(device):
        pl.semaphore_signal(barrier, inc=1, device_id=device, device_id_type=MESH)

    greet({"ctx": partner})
    for zz in (up, down):
        for hh in range(2):
            greet({"ctx": 2 * zz + hh})
    for step in range(1, 4):
        greet({"tp": (k + step) % 4})

    @pl.when(s < 3)
    def _():
        for zz in (z, up):
            for hh in range(2):
                greet({"section": s + 1, "ctx": 2 * zz + hh})

    pl.semaphore_wait(barrier, 8 + 4 * ((s + 3) // 4))

    def ring(j, to_right):
        target = {"ctx": 2 * (up if to_right else down) + h}
        after = j + 1 if to_right else (7 if j == 0 else j - 1)
        sem = j if to_right else 4 + (8 - j) % 8
        src, dst = (w_ref if j == 0 else wb.at[j]), wb.at[after]
        if after == 4:
            part = pl.ds(0 if to_right else 128, 128)
            src, dst = wb.at[j, :, part], wb.at[4, :, part]
        return remote(src, dst, ring_s.at[sem], ring_r.at[sem], target)

    rights = [ring(j, True) for j in (0, 1, 2, 3)]
    lefts = [ring(j, False) for j in (0, 7, 6, 5)]
    rights[0].start()
    lefts[0].start()

    own_rows = pl.ds(pl.multiple_of(BEFORE + 256 * h, 16), 256)
    other_rows = pl.ds(pl.multiple_of(BEFORE + 256 * (1 - h), 16), 256)
    own_g = pl.ds(pl.multiple_of(256 * h, 256), 256)
    other_g = pl.ds(pl.multiple_of(256 * (1 - h), 256), 256)
    saved = (u1_ref, u2_ref)
    grads = (g1_ref, gl_ref)

    local_w = pltpu.make_async_copy(w_ref, wb.at[0], loc.at[0])
    local_u = [pltpu.make_async_copy(saved[i], ue.at[i, :, own_rows], loc.at[1 + i]) for i in range(2)]
    local_g = [pltpu.make_async_copy(grads[i], ge.at[i, own_g], loc.at[3 + i]) for i in range(2)]
    send_u = [
        remote(saved[i], ue.at[i, :, own_rows], x_s.at[i], x_r.at[i], {"ctx": partner}) for i in range(2)
    ]
    send_g = [
        remote(grads[i], ge.at[i, own_g], x_s.at[2 + i], x_r.at[2 + i], {"ctx": partner})
        for i in range(2)
    ]
    get_u = [
        remote(saved[i], ue.at[i, :, other_rows], x_s.at[i], x_r.at[i], {"ctx": partner}) for i in range(2)
    ]
    get_g = [
        remote(grads[i], ge.at[i, other_g], x_s.at[2 + i], x_r.at[2 + i], {"ctx": partner})
        for i in range(2)
    ]

    def halo_before(i, hh):
        to = {"ctx": 2 * up + hh}
        u = saved[i]
        return [
            remote(u.at[pl.ds(1, 2), pl.ds(256 - BEFORE, BEFORE)], ue.at[i, pl.ds(1, 2), pl.ds(0, BEFORE)],
                   halo_s.at[i, 0, hh], halo_r.at[i, 0], to),
            remote(u.at[0, pl.ds(240, 16)], ue.at[i, 0, pl.ds(BEFORE - 16, 16)],
                   halo_s.at[i, 1, hh], halo_r.at[i, 1], to),
        ]

    def halo_after(i, hh):
        to = {"ctx": 2 * down + hh}
        u = saved[i]
        return [
            remote(u.at[0, pl.ds(0, AFTER)], ue.at[i, 0, pl.ds(BEFORE + GROUP, AFTER)],
                   halo_s.at[i, 0, hh], halo_r.at[i, 2], to),
            remote(u.at[pl.ds(1, 2), pl.ds(0, 32)], ue.at[i, pl.ds(1, 2), pl.ds(BEFORE + GROUP, 32)],
                   halo_s.at[i, 1, hh], halo_r.at[i, 3], to),
        ]

    def halo_g(i, hh):
        return remote(grads[i].at[pl.ds(0, AFTER)], ge.at[i, pl.ds(GROUP, AFTER)],
                      halo_s.at[i, 2, hh], halo_r.at[i, 4], {"ctx": 2 * down + hh})

    def start_halos(i):
        @pl.when(h == 1)
        def _():
            for hh in range(2):
                for copy in halo_before(i, hh):
                    copy.start()

        @pl.when(h == 0)
        def _():
            for hh in range(2):
                for copy in halo_after(i, hh):
                    copy.start()

    def end_halos(i):
        @pl.when(h == 1)
        def _():
            for hh in range(2):
                for copy in halo_before(i, hh):
                    copy.wait_send()

        @pl.when(h == 0)
        def _():
            for hh in range(2):
                for copy in halo_after(i, hh):
                    copy.wait_send()

    def receive_halos(i):
        for copy in halo_before(i, 0) + halo_after(i, 0):
            copy.wait_recv()

        @pl.when(z == 0)
        def _():
            ue[i, pl.ds(0, 3), pl.ds(BEFORE - 16, 16)] = jnp.zeros((3, 16, 1024), bf16)
            ue[i, pl.ds(1, 2), pl.ds(0, BEFORE - 16)] = jnp.zeros((2, BEFORE - 16, 1024), bf16)

    def clear_edge(i):
        @pl.when(z == 7)
        def _():
            ge[i, pl.ds(GROUP, AFTER)] = jnp.zeros((AFTER, 1024), bf16)

    local_u[0].start()
    local_g[0].start()
    send_u[0].start()
    send_g[0].start()
    start_halos(0)

    @pl.when(h == 0)
    def _():
        for hh in range(2):
            halo_g(0, hh).start()

    local_w.start()
    local_u[1].start()
    send_u[1].start()
    start_halos(1)

    @pl.when(last)
    def _():
        local_g[1].start()
        send_g[1].start()

        @pl.when(h == 0)
        def _():
            for hh in range(2):
                halo_g(1, hh).start()

    resp[...] = jnp.dot(
        fwd32_ref[...], long_ref[...], precision=lax.Precision.HIGHEST, preferred_element_type=f32
    )

    def columns(r):
        return pl.ds(pl.multiple_of(r * CHUNK, CHUNK), CHUNK)

    def features(i):
        def chunk(r, _):
            cols = columns(r)

            def short(m, x):
                total = x[16:] * short_ref[m, 0:1, cols]
                for tap in range(1, 7):
                    total += pltpu.roll(x, tap, 0)[16:] * short_ref[m, tap : tap + 1, cols]
                return total

            def tile(b, _):
                here = pl.ds(pl.multiple_of(b * TILE, TILE), TILE)
                wide = pl.ds(pl.multiple_of(b * TILE, TILE), TILE + 16)
                key = short(1, ue[i, 1, wide, cols].astype(f32))
                value = short(2, ue[i, 2, wide, cols].astype(f32))
                p1[here, cols] = key
                p2[here, cols] = value
                pr[here] = (key * value).astype(bf16)
                wide = pl.ds(pl.multiple_of(BEFORE - 16 + b * TILE, 16), TILE + 16)
                p0[here, cols] = short(0, ue[i, 0, wide, cols].astype(f32))
                return 0

            lax.fori_loop(0, REACH // TILE, tile, 0)
            real, imag = resp[:HALF, cols], resp[HALF:, cols]
            for b in range(4):
                mx[HALF * b : HALF * (b + 1), cols] = filtered(
                    fwd_ref[...], inv_ref[HALF:], pr[HALF * b : HALF * b + N], real, imag
                )
            mx[GROUP:KEPT, cols] = filtered(
                fwd_ref[:, :AFTER], inv_ref[HALF : HALF + 16], pr[GROUP:REACH], real, imag
            )
            return 0

        lax.fori_loop(0, 4, chunk, 0)

    def gradients(i):
        def chunk(r, _):
            cols = columns(r)

            def scale(b, _):
                here = pl.ds(pl.multiple_of(b * TILE, TILE), TILE)
                dm[here] = (ge[i, here, cols].astype(f32) * p0[here, cols]).astype(bf16)
                return 0

            lax.fori_loop(0, REACH // TILE, scale, 0)
            real, imag = resp[:HALF, cols], -resp[HALF:, cols]
            for b in range(5):
                rows = HALF if b < 4 else 16
                span = N if b < 4 else AFTER
                begin = HALF * b
                dproduct = filtered(
                    fwd_ref[:, :span], inv_ref[:rows], dm[begin : begin + span], real, imag
                )
                there = slice(begin, begin + rows)
                shifted = slice(begin + HALF, begin + HALF + rows)
                df[0, there] = ge[i, there, cols].astype(f32) * mx[there, cols]
                df[1, there] = dproduct * p2[shifted, cols]
                df[2, there] = dproduct * p1[shifted, cols]

            def tile(b, _):
                here = pl.ds(pl.multiple_of(b * TILE, TILE), TILE)
                wide = pl.ds(pl.multiple_of(b * TILE, TILE), TILE + 8)
                for m in range(3):
                    x = df[m, wide]
                    total = x[:TILE] * short_ref[m, 0:1, cols]
                    for tap in range(1, 7):
                        total += pltpu.roll(x, TILE + 8 - tap, 0)[:TILE] * short_ref[m, tap : tap + 1, cols]
                    di[m, here, cols] = total.astype(bf16)
                return 0

            lax.fori_loop(0, GROUP // TILE, tile, 0)
            return 0

        lax.fori_loop(0, 4, chunk, 0)

    def place(j):
        zt = (z + 8 - j) % 8
        return zt // 2, zt % 2

    def tp_copy(i, j):
        kt, q = place(j)
        return remote(pb.at[j], rb.at[i, k, q], tp_s.at[i, j], tp_r.at[i, k, q], {"tp": kt})

    def end_tp(i, j):
        kt, _ = place(j)

        @pl.when(kt != k)
        def _():
            tp_copy(i, j).wait_send()

    def multiply(i, lo, hi):
        def unit(n, _):
            odd = n % 2
            j = odd * ((n + 1) // 2) + (1 - odd) * ((8 - n // 2) % 8)
            if i == 1:
                end_tp(0, j)
            total = None
            for m in range(3):
                term = lax.dot_general(
                    di[m], wb[j, m], (((1,), (1,)), ((), ())), preferred_element_type=f32
                )
                total = term if total is None else total + term
            pb[j] = total.astype(bf16)
            kt, _q = place(j)

            @pl.when(kt != k)
            def _():
                tp_copy(i, j).start()

            return 0

        lax.fori_loop(lo, hi, unit, 0)

    def combine(i):
        for q in range(2):
            cols = columns(h + 2 * q)
            for step in range(1, 4):
                src = (k + step) % 4
                remote(pb.at[0], rb.at[i, src, q], tp_s.at[i, 0], tp_r.at[i, src, q], {"tp": src}).wait_recv()
            mine = (z + 8 - 2 * k - q) % 8

            def tile(b, _):
                here = pl.ds(pl.multiple_of(b * 64, 64), 64)
                total = ge[i, here, cols].astype(f32) + pb[mine, here].astype(f32)
                for step in range(1, 4):
                    total += rb[i, (k + step) % 4, q, here].astype(f32)
                sb[i, q, here] = total.astype(bf16)
                return 0

            lax.fori_loop(0, GROUP // 64, tile, 0)

    outs = (out1_ref, out2_ref)

    def finals(i, q):
        mine, theirs = columns(h + 2 * q), columns(1 - h + 2 * q)
        keep = pltpu.make_async_copy(sb.at[i, q, own_g], outs[i].at[:, mine], loc.at[5 + 2 * i + q])
        give = remote(sb.at[i, q, other_g], outs[i].at[:, mine], fin_s.at[i, q], fin_r.at[i, q], {"ctx": partner})
        take = remote(sb.at[i, q, other_g], outs[i].at[:, theirs], fin_s.at[i, q], fin_r.at[i, q], {"ctx": partner})
        return keep, give, take

    def relay(q, hh):
        r = h + 2 * q
        to = {"section": lax.rem(s + 3, 4), "ctx": 2 * z + hh}
        edge_to = {"section": lax.rem(s + 3, 4), "ctx": 2 * down + hh}
        return (
            remote(sb.at[0, q], ge.at[1, pl.ds(0, GROUP), columns(r)], main_s.at[q, hh], main_r.at[r], to),
            remote(sb.at[0, q, pl.ds(0, AFTER)], ge.at[1, pl.ds(GROUP, AFTER), columns(r)],
                   edge_s.at[q, hh], edge_r.at[r], edge_to),
        )

    rights[0].wait_recv()
    rights[1].start()
    lefts[0].wait_recv()
    lefts[1].start()
    local_u[0].wait()
    local_g[0].wait()
    get_u[0].wait_recv()
    receive_halos(0)
    features(0)
    rights[1].wait_recv()
    rights[2].start()
    lefts[1].wait_recv()
    lefts[2].start()
    get_g[0].wait_recv()
    halo_g(0, 0).wait_recv()
    clear_edge(0)
    gradients(0)
    local_u[1].wait()
    get_u[1].wait_recv()
    receive_halos(1)
    features(1)
    local_w.wait()
    multiply(0, 0, 5)
    rights[2].wait_recv()
    rights[3].start()
    lefts[2].wait_recv()
    lefts[3].start()
    multiply(0, 5, 7)
    rights[3].wait_recv()
    lefts[3].wait_recv()
    multiply(0, 7, 8)
    combine(0)

    @pl.when(s > 0)
    def _():
        for q in range(2):
            for hh in range(2):
                for copy in relay(q, hh):
                    copy.start()

    for q in range(2):
        keep, give, _ = finals(0, q)
        keep.start()
        give.start()

    @pl.when(last)
    def _():
        local_g[1].wait()
        get_g[1].wait_recv()
        halo_g(1, 0).wait_recv()

    @pl.when(s < 3)
    def _():
        for r in range(4):
            remote(sb.at[0, 0], ge.at[1, pl.ds(0, GROUP), columns(r)], main_s.at[0, 0], main_r.at[r],
                   {"ctx": partner}).wait_recv()
            remote(sb.at[0, 0, pl.ds(0, AFTER)], ge.at[1, pl.ds(GROUP, AFTER), columns(r)], edge_s.at[0, 0],
                   edge_r.at[r], {"ctx": partner}).wait_recv()

    clear_edge(1)
    gradients(1)
    multiply(1, 0, 8)
    combine(1)
    for q in range(2):
        keep, give, _ = finals(1, q)
        keep.start()
        give.start()

    for copy in rights + lefts:
        copy.wait_send()
    for i in range(2):
        send_u[i].wait_send()
        end_halos(i)
    send_g[0].wait_send()

    @pl.when(h == 0)
    def _():
        for hh in range(2):
            halo_g(0, hh).wait_send()

    @pl.when(last)
    def _():
        send_g[1].wait_send()

        @pl.when(h == 0)
        def _():
            for hh in range(2):
                halo_g(1, hh).wait_send()

    @pl.when(s > 0)
    def _():
        for q in range(2):
            for hh in range(2):
                for copy in relay(q, hh):
                    copy.wait_send()

    def finish(j, _):
        end_tp(1, j)
        return 0

    lax.fori_loop(0, 8, finish, 0)
    for i in range(2):
        for q in range(2):
            keep, give, take = finals(i, q)
            keep.wait()
            give.wait_send()
            take.wait_recv()


def body(
    in_weights, short_taps, long_taps, first_saved, second_saved, first_cotangent, last_cotangent
):
    anywhere = pl.BlockSpec(memory_space=pl.ANY)
    vmem = pl.BlockSpec(memory_space=pltpu.VMEM)
    dma = pltpu.SemaphoreType.DMA
    first, second = pl.pallas_call(
        kernel,
        out_shape=(jax.ShapeDtypeStruct((256, 1024), bf16),) * 2,
        in_specs=[anywhere, vmem, vmem, anywhere, anywhere, anywhere, anywhere, vmem, vmem, vmem],
        out_specs=(anywhere, anywhere),
        scratch_shapes=[
            pltpu.VMEM((8, 3, 256, 1024), bf16),
            pltpu.VMEM((2, 3, ROWS, 1024), bf16),
            pltpu.VMEM((2, REACH, 1024), bf16),
            pltpu.VMEM((REACH, 1024), f32),
            pltpu.VMEM((REACH, 1024), f32),
            pltpu.VMEM((REACH, 1024), f32),
            pltpu.VMEM((KEPT, 1024), f32),
            pltpu.VMEM((3, GROUP, 1024), bf16),
            pltpu.VMEM((8, GROUP, 256), bf16),
            pltpu.VMEM((2, 4, 2, GROUP, 256), bf16),
            pltpu.VMEM((2, 2, GROUP, 256), bf16),
            pltpu.VMEM((N, 1024), f32),
            pltpu.VMEM((REACH, CHUNK), bf16),
            pltpu.VMEM((REACH, CHUNK), bf16),
            pltpu.VMEM((3, KEPT, CHUNK), f32),
            dma((8,)), dma((8,)), dma((4,)), dma((4,)), dma((9,)),
            dma((2, 3, 2)), dma((2, 5)), dma((2, 8)), dma((2, 4, 2)),
            dma((2, 2)), dma((4,)), dma((2, 2)), dma((4,)), dma((2, 2)), dma((2, 2)),
        ],
        compiler_params=pltpu.CompilerParams(
            collective_id=0, has_side_effects=True, vmem_limit_bytes=60 * 1024 * 1024
        ),
    )(
        in_weights[0], short_taps[0], long_taps[0], first_saved[0], second_saved[0],
        first_cotangent[0], last_cotangent,
        FORWARD.astype(bf16), INVERSE.astype(bf16), FORWARD[:, :HALF],
    )
    return first[None], second[None]


def solution(mesh):
    in_specs = (
        P("section", None, "ctx", "tp"),
        P("section", None, None, "tp"),
        P("section", None, "tp"),
        P("section", None, "ctx", "tp"),
        P("section", None, "ctx", "tp"),
        P("section", "ctx", "tp"),
        P("ctx", "tp"),
    )
    out_specs = (P("section", "ctx", "tp"), P("section", "ctx", "tp"))
    return jax.shard_map(body, mesh=mesh, in_specs=in_specs, out_specs=out_specs, check_vma=False)
```

profile of v0, /device:TPU:1, one launch (start us, length us, event | category | flops | bytes accessed | tf_op | source)
XLA Modules:
  0.0 258.7 jit_solution(6561187124768350837)
XLA Ops:
  0.6 1.6 copy.14
  2.2 252.8 %shard_map.113 = (bf16[256,1024]{1,0:T(8,128)(2,1)}, bf16[256,1024]{1,0:T(8,128)(2,1)}) custom-call(bf16[3,256,1024]{2,1,0:T(8,128)(2,1)} %bitcast.10, f32[3,7,1024]{2,1,0:T(8,128)} %bitcast.17, f32[128,1024]{1,0:T(8,128)} %bitcast.13, bf16[3,256,1024]{2,1,0:T(8,128)(2,1)} %bitcast.11, bf16[3,256,1024]{2,1,0:T(8,128)(2,1)} %bitcast.12, ...), custom_call_target="tpu_custom_call" | custom-call | tf_op jit(solution)/shard_map/pallas_call | solution.py:491
  255.0 1.9 copy.17
  256.9 1.9 copy.18
where the time goes:
time: 261 us; the launch traced here: 259 us
  Pallas kernels  253 us (97%)
  local copies, waits for them, and re-layouts  5.29 us (2%)
    pallas_call x1, Pallas kernels, body(): pl.pallas_call(kernel, out_shape=(jax.ShapeDtypeStruct((256, 1024), bf16)...  253 us
    unnamed x3, local copies, waits for them, and re-layouts  5.29 us

commit v1 on v0

--- a/solution.py
+++ b/solution.py
@@ -19,6 +19,7 @@
 KEPT = GROUP + 16
 CHUNK = 256
 TILE = 32
+FAR = 224
 f32 = jnp.float32
 bf16 = jnp.bfloat16
 
@@ -48,9 +49,9 @@
 def kernel(
     w_ref, short_ref, long_ref, u1_ref, u2_ref, g1_ref, gl_ref, fwd_ref, inv_ref, fwd32_ref,
     out1_ref, out2_ref,
-    wb, ue, ge, p0, p1, p2, mx, di, pb, rb, sb, resp, pr, dm, df,
-    ring_s, ring_r, x_s, x_r, loc, halo_s, halo_r, tp_s, tp_r, main_s, main_r, edge_s, edge_r,
-    fin_s, fin_r,
+    wb, ue, ge, p0, p1, p2, mx, di, pb, rb, tb, sb, resp, pr, dm, df,
+    ring_s, ring_r, x_s, x_r, loc, halo_s, halo_r, pass_s, tp_s, tp_r, sum_s, sum_r, hop_r, main_s, main_r,
+    edge_s, edge_r, fin_s, fin_r,
 ):
     s = lax.axis_index("section")
     c = lax.axis_index("ctx")
@@ -86,20 +87,48 @@
 
     pl.semaphore_wait(barrier, 8 + 4 * ((s + 3) // 4))
 
-    def ring(j, to_right):
+    def ring(to_right, step, piece, rows=None):
         target = {"ctx": 2 * (up if to_right else down) + h}
-        after = j + 1 if to_right else (7 if j == 0 else j - 1)
-        sem = j if to_right else 4 + (8 - j) % 8
-        src, dst = (w_ref if j == 0 else wb.at[j]), wb.at[after]
-        if after == 4:
-            part = pl.ds(0 if to_right else 128, 128)
-            src, dst = wb.at[j, :, part], wb.at[4, :, part]
-        return remote(src, dst, ring_s.at[sem], ring_r.at[sem], target)
-
-    rights = [ring(j, True) for j in (0, 1, 2, 3)]
-    lefts = [ring(j, False) for j in (0, 7, 6, 5)]
-    rights[0].start()
-    lefts[0].start()
+        rows = rows or (128 * piece, 128)
+        part = pl.ds(*rows)
+        source = step if to_right else (8 - step) % 8
+        dest = step + 1 if to_right else 7 - step
+        src = w_ref.at[:, part] if step == 0 else wb.at[source, :, part]
+        way = 0 if to_right else 1
+        return remote(src, wb.at[dest, :, part], ring_s.at[way, step, piece], ring_r.at[way, step, piece], target)
+
+    def ends(hh, piece):
+        if hh == 0:
+            return ring(True, 3, 0) if piece == 0 else ring(True, 3, 1, (128, FAR - 128))
+        return ring(False, 3, 1) if piece == 1 else ring(False, 3, 0, (256 - FAR, FAR - 128))
+
+    def short_end(hh):
+        return ring(False, 3, 1, (FAR, 256 - FAR)) if hh == 0 else ring(True, 3, 0, (0, 256 - FAR))
+
+    def by_column(act):
+        for hh in range(2):
+            pl.when(h == hh)(functools.partial(act, hh))
+
+    def hand_on(step, turn):
+        def act(hh):
+            piece = turn if hh == 0 else 1 - turn
+            for to_right in ((False, True) if hh == 1 else (True, False)):
+                ring(to_right, step, piece).wait_recv()
+                if step < 2:
+                    ring(to_right, step + 1, piece).start()
+                elif to_right == (hh == 0):
+                    ends(hh, piece).start()
+                elif turn == 1:
+                    short_end(hh).start()
+
+        by_column(act)
+
+    def begin(hh):
+        for turn in range(2):
+            for to_right in (True, False):
+                ring(to_right, 0, turn if hh == 0 else 1 - turn).start()
+
+    by_column(begin)
 
     own_rows = pl.ds(pl.multiple_of(BEFORE + 256 * h, 16), 256)
     other_rows = pl.ds(pl.multiple_of(BEFORE + 256 * (1 - h), 16), 256)
@@ -126,95 +155,104 @@
         for i in range(2)
     ]
 
-    def halo_before(i, hh):
-        to = {"ctx": 2 * up + hh}
-        u = saved[i]
+    def before_parts(i):
         return [
-            remote(u.at[pl.ds(1, 2), pl.ds(256 - BEFORE, BEFORE)], ue.at[i, pl.ds(1, 2), pl.ds(0, BEFORE)],
-                   halo_s.at[i, 0, hh], halo_r.at[i, 0], to),
-            remote(u.at[0, pl.ds(240, 16)], ue.at[i, 0, pl.ds(BEFORE - 16, 16)],
-                   halo_s.at[i, 1, hh], halo_r.at[i, 1], to),
+            (saved[i].at[pl.ds(1, 2), pl.ds(256 - BEFORE, BEFORE)], ue.at[i, pl.ds(1, 2), pl.ds(0, BEFORE)], 0),
+            (saved[i].at[0, pl.ds(240, 16)], ue.at[i, 0, pl.ds(BEFORE - 16, 16)], 1),
         ]
 
-    def halo_after(i, hh):
-        to = {"ctx": 2 * down + hh}
-        u = saved[i]
+    def after_parts(i):
         return [
-            remote(u.at[0, pl.ds(0, AFTER)], ue.at[i, 0, pl.ds(BEFORE + GROUP, AFTER)],
-                   halo_s.at[i, 0, hh], halo_r.at[i, 2], to),
-            remote(u.at[pl.ds(1, 2), pl.ds(0, 32)], ue.at[i, pl.ds(1, 2), pl.ds(BEFORE + GROUP, 32)],
-                   halo_s.at[i, 1, hh], halo_r.at[i, 3], to),
+            (saved[i].at[0, pl.ds(0, AFTER)], ue.at[i, 0, pl.ds(BEFORE + GROUP, AFTER)], 2),
+            (saved[i].at[pl.ds(1, 2), pl.ds(0, 32)], ue.at[i, pl.ds(1, 2), pl.ds(BEFORE + GROUP, 32)], 3),
         ]
 
-    def halo_g(i, hh):
-        return remote(grads[i].at[pl.ds(0, AFTER)], ge.at[i, pl.ds(GROUP, AFTER)],
-                      halo_s.at[i, 2, hh], halo_r.at[i, 4], {"ctx": 2 * down + hh})
-
-    def start_halos(i):
+    def grad_parts(i):
+        return [(grads[i].at[pl.ds(0, AFTER)], ge.at[i, pl.ds(GROUP, AFTER)], 4)]
+
+    def along(i, parts, to):
+        return [remote(src, dst, halo_s.at[i, n], halo_r.at[i, n], {"ctx": to}) for src, dst, n in parts]
+
+    def onward(i, parts):
+        return [remote(dst, dst, pass_s.at[i, n], halo_r.at[i, n], {"ctx": partner}) for _, dst, n in parts]
+
+    def start_halos(i, with_u, with_g):
         @pl.when(h == 1)
         def _():
-            for hh in range(2):
-                for copy in halo_before(i, hh):
+            if with_u:
+                for copy in along(i, before_parts(i), 2 * up + 1):
                     copy.start()
 
         @pl.when(h == 0)
         def _():
-            for hh in range(2):
-                for copy in halo_after(i, hh):
+            for copy in along(i, after_parts(i) * with_u + grad_parts(i) * with_g, 2 * down):
+                copy.start()
+
+    def end_halos(i, with_u, with_g):
+        @pl.when(h == 1)
+        def _():
+            if with_u:
+                for copy in along(i, before_parts(i), 2 * up + 1) + onward(i, before_parts(i)):
+                    copy.wait_send()
+
+        @pl.when(h == 0)
+        def _():
+            parts = after_parts(i) * with_u + grad_parts(i) * with_g
+            for copy in along(i, parts, 2 * down) + onward(i, parts):
+                copy.wait_send()
+
+    def pass_halos(i, with_u, with_g):
+        @pl.when(h == 1)
+        def _():
+            if with_u:
+                for copy in along(i, before_parts(i), 2 * up + 1):
+                    copy.wait_recv()
+
+                @pl.when(z == 0)
+                def _():
+                    ue[i, pl.ds(0, 3), pl.ds(BEFORE - 16, 16)] = jnp.zeros((3, 16, 1024), bf16)
+                    ue[i, pl.ds(1, 2), pl.ds(0, BEFORE - 16)] = jnp.zeros((2, BEFORE - 16, 1024), bf16)
+
+                for copy in onward(i, before_parts(i)):
                     copy.start()
 
-    def end_halos(i):
+        @pl.when(h == 0)
+        def _():
+            parts = after_parts(i) * with_u + grad_parts(i) * with_g
+            for copy in along(i, parts, 2 * down):
+                copy.wait_recv()
+
+            if with_g:
+                @pl.when(z == 7)
+                def _():
+                    ge[i, pl.ds(GROUP, AFTER)] = jnp.zeros((AFTER, 1024), bf16)
+
+            for copy in onward(i, parts):
+                copy.start()
+
+    def receive_halos(i, with_u, with_g):
         @pl.when(h == 1)
         def _():
-            for hh in range(2):
-                for copy in halo_before(i, hh):
-                    copy.wait_send()
+            for copy in onward(i, after_parts(i) * with_u + grad_parts(i) * with_g):
+                copy.wait_recv()
 
         @pl.when(h == 0)
         def _():
-            for hh in range(2):
-                for copy in halo_after(i, hh):
-                    copy.wait_send()
-
-    def receive_halos(i):
-        for copy in halo_before(i, 0) + halo_after(i, 0):
-            copy.wait_recv()
-
-        @pl.when(z == 0)
-        def _():
-            ue[i, pl.ds(0, 3), pl.ds(BEFORE - 16, 16)] = jnp.zeros((3, 16, 1024), bf16)
-            ue[i, pl.ds(1, 2), pl.ds(0, BEFORE - 16)] = jnp.zeros((2, BEFORE - 16, 1024), bf16)
-
-    def clear_edge(i):
-        @pl.when(z == 7)
-        def _():
-            ge[i, pl.ds(GROUP, AFTER)] = jnp.zeros((AFTER, 1024), bf16)
+            if with_u:
+                for copy in onward(i, before_parts(i)):
+                    copy.wait_recv()
 
     local_u[0].start()
     local_g[0].start()
     send_u[0].start()
     send_g[0].start()
-    start_halos(0)
-
-    @pl.when(h == 0)
-    def _():
-        for hh in range(2):
-            halo_g(0, hh).start()
-
+    start_halos(0, True, True)
     local_w.start()
     local_u[1].start()
-    send_u[1].start()
-    start_halos(1)
 
     @pl.when(last)
     def _():
         local_g[1].start()
-        send_g[1].start()
-
-        @pl.when(h == 0)
-        def _():
-            for hh in range(2):
-                halo_g(1, hh).start()
 
     resp[...] = jnp.dot(
         fwd32_ref[...], long_ref[...], precision=lax.Precision.HIGHEST, preferred_element_type=f32
@@ -258,9 +296,25 @@
 
         lax.fori_loop(0, 4, chunk, 0)
 
+    def take_relay(r):
+        cols = columns(r)
+
+        @pl.when(s < 3)
+        def _():
+            remote(sb.at[0, 0], ge.at[1, pl.ds(0, GROUP), cols], main_s.at[0, 0], main_r.at[r],
+                   {"ctx": partner}).wait_recv()
+            remote(sb.at[0, 0, pl.ds(0, AFTER)], ge.at[1, pl.ds(GROUP, AFTER), cols], edge_s.at[0, 0],
+                   edge_r.at[r], {"ctx": partner}).wait_recv()
+
+            @pl.when(z == 7)
+            def _():
+                ge[1, pl.ds(GROUP, AFTER), cols] = jnp.zeros((AFTER, CHUNK), bf16)
+
     def gradients(i):
         def chunk(r, _):
             cols = columns(r)
+            if i == 1:
+                take_relay(r)
 
             def scale(b, _):
                 here = pl.ds(pl.multiple_of(b * TILE, TILE), TILE)
@@ -282,18 +336,21 @@
                 df[1, there] = dproduct * p2[shifted, cols]
                 df[2, there] = dproduct * p1[shifted, cols]
 
-            def tile(b, _):
-                here = pl.ds(pl.multiple_of(b * TILE, TILE), TILE)
-                wide = pl.ds(pl.multiple_of(b * TILE, TILE), TILE + 8)
+            def tile(n, _):
+                b, side = n // 2, n % 2
+                here = pl.ds(pl.multiple_of(b * HALF, HALF), HALF)
+                wide = pl.ds(pl.multiple_of(b * HALF, HALF), HALF + 8)
+                part = pl.ds(pl.multiple_of(side * 128, 128), 128)
+                there = pl.ds(pl.multiple_of(r * CHUNK + side * 128, 128), 128)
                 for m in range(3):
-                    x = df[m, wide]
-                    total = x[:TILE] * short_ref[m, 0:1, cols]
+                    x = df[m, wide, part]
+                    total = x[:HALF] * short_ref[m, 0:1, there]
                     for tap in range(1, 7):
-                        total += pltpu.roll(x, TILE + 8 - tap, 0)[:TILE] * short_ref[m, tap : tap + 1, cols]
-                    di[m, here, cols] = total.astype(bf16)
+                        total += pltpu.roll(x, HALF + 8 - tap, 0)[:HALF] * short_ref[m, tap : tap + 1, there]
+                    di[m, here, there] = total.astype(bf16)
                 return 0
 
-            lax.fori_loop(0, GROUP // TILE, tile, 0)
+            lax.fori_loop(0, 8, tile, 0)
             return 0
 
         lax.fori_loop(0, 4, chunk, 0)
@@ -302,57 +359,115 @@
         zt = (z + 8 - j) % 8
         return zt // 2, zt % 2
 
-    def tp_copy(i, j):
+    def half_copy(j, half):
         kt, q = place(j)
-        return remote(pb.at[j], rb.at[i, k, q], tp_s.at[i, j], tp_r.at[i, k, q], {"tp": kt})
-
-    def end_tp(i, j):
+        cols = pl.ds(128 * half if isinstance(half, int) else pl.multiple_of(128 * half, 128), 128)
+        return remote(pb.at[j, :, cols], rb.at[0, k, q, :, cols], tp_s.at[j, half], tp_r.at[k, q, half], {"tp": kt})
+
+    def end_first(j):
         kt, _ = place(j)
 
         @pl.when(kt != k)
         def _():
-            tp_copy(i, j).wait_send()
-
-    def multiply(i, lo, hi):
+            for half in range(2):
+                half_copy(j, half).wait_send()
+
+    def end_second(j):
+        kt, q = place(j)
+
+        @pl.when(kt != k)
+        def _():
+            remote(pb.at[j], rb.at[1, k, q], sum_s.at[j], sum_r.at[k, q], {"tp": kt}).wait_send()
+
+    def product(j):
+        total = None
+        for m in range(3):
+            term = lax.dot_general(di[m], wb[j, m], (((1,), (1,)), ((), ())), preferred_element_type=f32)
+            total = term if total is None else total + term
+        return total.astype(bf16)
+
+    def multiply_first(lo, hi):
         def unit(n, _):
             odd = n % 2
             j = odd * ((n + 1) // 2) + (1 - odd) * ((8 - n // 2) % 8)
-            if i == 1:
-                end_tp(0, j)
-            total = None
-            for m in range(3):
-                term = lax.dot_general(
-                    di[m], wb[j, m], (((1,), (1,)), ((), ())), preferred_element_type=f32
-                )
-                total = term if total is None else total + term
-            pb[j] = total.astype(bf16)
+            pb[j] = product(j)
             kt, _q = place(j)
 
             @pl.when(kt != k)
             def _():
-                tp_copy(i, j).start()
+                for half in range(2):
+                    half_copy(j, half).start()
 
             return 0
 
         lax.fori_loop(lo, hi, unit, 0)
 
-    def combine(i):
-        for q in range(2):
-            cols = columns(h + 2 * q)
-            for step in range(1, 4):
-                src = (k + step) % 4
-                remote(pb.at[0], rb.at[i, src, q], tp_s.at[i, 0], tp_r.at[i, src, q], {"tp": src}).wait_recv()
-            mine = (z + 8 - 2 * k - q) % 8
-
-            def tile(b, _):
-                here = pl.ds(pl.multiple_of(b * 64, 64), 64)
-                total = ge[i, here, cols].astype(f32) + pb[mine, here].astype(f32)
-                for step in range(1, 4):
-                    total += rb[i, (k + step) % 4, q, here].astype(f32)
-                sb[i, q, here] = total.astype(bf16)
-                return 0
-
-            lax.fori_loop(0, GROUP // 64, tile, 0)
+    def multiply_half(turn):
+        half = turn * (1 - h) + (1 - turn) * h
+        rows = pl.ds(pl.multiple_of(128 * half, 128), 128)
+        total = None
+        for m in range(3):
+            term = lax.dot_general(
+                di[m], wb[4, m, rows], (((1,), (1,)), ((), ())), preferred_element_type=f32
+            )
+            total = term if total is None else total + term
+        pb[4, :, rows] = total.astype(bf16)
+        kt, _ = place(4)
+
+        @pl.when(kt != k)
+        def _():
+            half_copy(4, half).start()
+
+    def multiply_second():
+        def unit(n, _):
+            odd, pair = n % 2, n // 2
+            away = jnp.where(pair == 0, 2, jnp.where(pair == 2, 0, 1 + 2 * odd))
+            q = jnp.where(pair == 1, 1 - odd, odd)
+            target = (k + away) % 4
+            j = (z + 8 - 2 * target - q) % 8
+            end_first(j)
+            pb[j] = product(j)
+
+            @pl.when(n < 2)
+            def _():
+                remote(pb.at[j], tb.at[q], sum_s.at[j], hop_r.at[q], {"tp": (k + 1 + 2 * q) % 4}).start()
+
+            @pl.when(n >= 6)
+            def _():
+                remote(pb.at[j], tb.at[q], sum_s.at[j], hop_r.at[q], {"tp": target}).wait_recv()
+                pb[j] = (pb[j].astype(f32) + tb[q].astype(f32)).astype(bf16)
+
+            @pl.when((pair == 1) | (pair == 3))
+            def _():
+                remote(pb.at[j], rb.at[1, k, q], sum_s.at[j], sum_r.at[k, q], {"tp": target}).start()
+
+            return 0
+
+        lax.fori_loop(0, 8, unit, 0)
+
+    def combine(i, q):
+        cols = columns(h + 2 * q)
+        steps = (1, 2, 3) if i == 0 else (1, 3)
+        for step in steps:
+            src = (k + step) % 4
+            if i == 1:
+                remote(pb.at[0], rb.at[1, src, q], sum_s.at[0], sum_r.at[src, q], {"tp": src}).wait_recv()
+                continue
+            for half in range(2):
+                part = pl.ds(128 * half, 128)
+                remote(pb.at[0, :, part], rb.at[0, src, q, :, part], tp_s.at[0, half],
+                       tp_r.at[src, q, half], {"tp": src}).wait_recv()
+        mine = (z + 8 - 2 * k - q) % 8
+
+        def tile(b, _):
+            here = pl.ds(pl.multiple_of(b * 64, 64), 64)
+            total = ge[i, here, cols].astype(f32) + pb[mine, here].astype(f32)
+            for step in steps:
+                total += rb[i, (k + step) % 4, q, here].astype(f32)
+            sb[i, q, here] = total.astype(bf16)
+            return 0
+
+        lax.fori_loop(0, GROUP // 64, tile, 0)
 
     outs = (out1_ref, out2_ref)
 
@@ -373,104 +488,105 @@
                    edge_s.at[q, hh], edge_r.at[r], edge_to),
         )
 
-    rights[0].wait_recv()
-    rights[1].start()
-    lefts[0].wait_recv()
-    lefts[1].start()
+    hand_on(0, 0)
+    hand_on(0, 1)
+    pass_halos(0, True, True)
     local_u[0].wait()
     local_g[0].wait()
     get_u[0].wait_recv()
-    receive_halos(0)
+    get_g[0].wait_recv()
+    send_u[1].start()
+    start_halos(1, True, False)
+
+    @pl.when(last)
+    def _():
+        send_g[1].start()
+        start_halos(1, False, True)
+
+    receive_halos(0, True, True)
+    hand_on(1, 0)
     features(0)
-    rights[1].wait_recv()
-    rights[2].start()
-    lefts[1].wait_recv()
-    lefts[2].start()
-    get_g[0].wait_recv()
-    halo_g(0, 0).wait_recv()
-    clear_edge(0)
+    hand_on(1, 1)
     gradients(0)
+    local_w.wait()
+    multiply_first(0, 5)
+    pass_halos(1, True, False)
+
+    @pl.when(last)
+    def _():
+        pass_halos(1, False, True)
+
+    hand_on(2, 0)
     local_u[1].wait()
     get_u[1].wait_recv()
-    receive_halos(1)
+    receive_halos(1, True, False)
     features(1)
-    local_w.wait()
-    multiply(0, 0, 5)
-    rights[2].wait_recv()
-    rights[3].start()
-    lefts[2].wait_recv()
-    lefts[3].start()
-    multiply(0, 5, 7)
-    rights[3].wait_recv()
-    lefts[3].wait_recv()
-    multiply(0, 7, 8)
-    combine(0)
-
-    @pl.when(s > 0)
+    hand_on(2, 1)
+
+    @pl.when(last)
     def _():
-        for q in range(2):
-            for hh in range(2):
-                for copy in relay(q, hh):
-                    copy.start()
+        local_g[1].wait()
+        get_g[1].wait_recv()
+        receive_halos(1, False, True)
+
+    multiply_first(5, 7)
+    by_column(lambda hh: ends(hh, hh).wait_recv())
+    multiply_half(0)
+
+    def arrive(hh):
+        ends(hh, 1 - hh).wait_recv()
+        short_end(hh).wait_recv()
+
+    by_column(arrive)
+    multiply_half(1)
+    for q in range(2):
+        combine(0, q)
+
+        @pl.when(s > 0)
+        def _():
+            for copy in relay(q, 0) + relay(q, 1):
+                copy.start()
 
     for q in range(2):
         keep, give, _ = finals(0, q)
         keep.start()
         give.start()
 
-    @pl.when(last)
-    def _():
-        local_g[1].wait()
-        get_g[1].wait_recv()
-        halo_g(1, 0).wait_recv()
-
-    @pl.when(s < 3)
-    def _():
-        for r in range(4):
-            remote(sb.at[0, 0], ge.at[1, pl.ds(0, GROUP), columns(r)], main_s.at[0, 0], main_r.at[r],
-                   {"ctx": partner}).wait_recv()
-            remote(sb.at[0, 0, pl.ds(0, AFTER)], ge.at[1, pl.ds(GROUP, AFTER), columns(r)], edge_s.at[0, 0],
-                   edge_r.at[r], {"ctx": partner}).wait_recv()
-
-    clear_edge(1)
     gradients(1)
-    multiply(1, 0, 8)
-    combine(1)
+    multiply_second()
     for q in range(2):
+        combine(1, q)
         keep, give, _ = finals(1, q)
+        give.start()
         keep.start()
-        give.start()
-
-    for copy in rights + lefts:
-        copy.wait_send()
+
+    def sent(hh):
+        for to_right in (True, False):
+            for step in range(3):
+                for piece in range(2):
+                    ring(to_right, step, piece).wait_send()
+        for copy in (ends(hh, 0), ends(hh, 1), short_end(hh)):
+            copy.wait_send()
+
+    by_column(sent)
     for i in range(2):
         send_u[i].wait_send()
-        end_halos(i)
+        end_halos(i, True, i == 0)
     send_g[0].wait_send()
-
-    @pl.when(h == 0)
-    def _():
-        for hh in range(2):
-            halo_g(0, hh).wait_send()
 
     @pl.when(last)
     def _():
         send_g[1].wait_send()
-
-        @pl.when(h == 0)
-        def _():
-            for hh in range(2):
-                halo_g(1, hh).wait_send()
+        end_halos(1, False, True)
 
     @pl.when(s > 0)
     def _():
         for q in range(2):
-            for hh in range(2):
-                for copy in relay(q, hh):
-                    copy.wait_send()
+            for copy in relay(q, 0) + relay(q, 1):
+                copy.wait_send()
 
     def finish(j, _):
-        end_tp(1, j)
+        end_second(j)
         return 0
 
     lax.fori_loop(0, 8, finish, 0)
@@ -504,13 +620,14 @@
             pltpu.VMEM((3, GROUP, 1024), bf16),
             pltpu.VMEM((8, GROUP, 256), bf16),
             pltpu.VMEM((2, 4, 2, GROUP, 256), bf16),
+            pltpu.VMEM((2, GROUP, 256), bf16),
             pltpu.VMEM((2, 2, GROUP, 256), bf16),
             pltpu.VMEM((N, 1024), f32),
             pltpu.VMEM((REACH, CHUNK), bf16),
             pltpu.VMEM((REACH, CHUNK), bf16),
             pltpu.VMEM((3, KEPT, CHUNK), f32),
-            dma((8,)), dma((8,)), dma((4,)), dma((4,)), dma((9,)),
-            dma((2, 3, 2)), dma((2, 5)), dma((2, 8)), dma((2, 4, 2)),
+            dma((2, 4, 2)), dma((2, 4, 2)), dma((4,)), dma((4,)), dma((9,)),
+            dma((2, 5)), dma((2, 5)), dma((2, 5)), dma((8, 2)), dma((4, 2, 2)), dma((8,)), dma((4, 2)), dma((2,)),
             dma((2, 2)), dma((4,)), dma((2, 2)), dma((4,)), dma((2, 2)), dma((2, 2)),
         ],
         compiler_params=pltpu.CompilerParams(

time: 261 us -> 217 us (0.83)
  Pallas kernels: 253 us -> 211 us
    pallas_call x1, Pallas kernels: 253 us -> 211 us  [body(): pl.pallas_call(kernel, out_shape=(jax.ShapeDtypeStruct((256, 1024), bf16)...]
where the time goes in v1:
time: 217 us
  Pallas kernels  211 us (97%)
  local copies, waits for them, and re-layouts  5.29 us (2%)
    pallas_call x1, Pallas kernels, body(): pl.pallas_call(kernel, out_shape=(jax.ShapeDtypeStruct((256, 1024), bf16)...  211 us
    unnamed x3, local copies, waits for them, and re-layouts  5.29 us

profile of v1, /device:TPU:1, one launch (start us, length us, event | category | flops | bytes accessed | tf_op | source)
XLA Modules:
  0.0 216.9 jit_solution(16452573021474093218)
XLA Ops:
  0.6 1.6 copy.14
  2.2 210.9 %shard_map.113 = (bf16[256,1024]{1,0:T(8,128)(2,1)}, bf16[256,1024]{1,0:T(8,128)(2,1)}) custom-call(bf16[3,256,1024]{2,1,0:T(8,128)(2,1)} %bitcast.10, f32[3,7,1024]{2,1,0:T(8,128)} %bitcast.17, f32[128,1024]{1,0:T(8,128)} %bitcast.13, bf16[3,256,1024]{2,1,0:T(8,128)(2,1)} %bitcast.11, bf16[3,256,1024]{2,1,0:T(8,128)(2,1)} %bitcast.12, ...), custom_call_target="tpu_custom_call" | custom-call | tf_op jit(solution)/shard_map/pallas_call | solution.py:607
  213.1 1.9 copy.17
  215.0 1.9 copy.18

commit v2 on v1

--- a/solution.py
+++ b/solution.py
@@ -547,12 +547,11 @@
             for copy in relay(q, 0) + relay(q, 1):
                 copy.start()
 
+    gradients(1)
     for q in range(2):
         keep, give, _ = finals(0, q)
         keep.start()
         give.start()
-
-    gradients(1)
     multiply_second()
     for q in range(2):
         combine(1, q)

time: 217 us -> 215 us (level); the launches traced: 217 us -> 212 us
  Pallas kernels: 211 us -> 206 us
    pallas_call x1, Pallas kernels: 211 us -> 206 us  [body(): pl.pallas_call(kernel, out_shape=(jax.ShapeDtypeStruct((256, 1024), bf16)...]
where the time goes in v2:
time: 215 us; the launch traced here: 212 us
  Pallas kernels  206 us (96%)
  local copies, waits for them, and re-layouts  5.29 us (2%)
    pallas_call x1, Pallas kernels, body(): pl.pallas_call(kernel, out_shape=(jax.ShapeDtypeStruct((256, 1024), bf16)...  206 us
    unnamed x3, local copies, waits for them, and re-layouts  5.29 us

profile of v2, /device:TPU:1, one launch (start us, length us, event | category | flops | bytes accessed | tf_op | source)
XLA Modules:
  0.0 212.4 jit_solution(14543268941995526472)
XLA Ops:
  0.6 1.6 copy.14
  2.2 206.5 %shard_map.113 = (bf16[256,1024]{1,0:T(8,128)(2,1)}, bf16[256,1024]{1,0:T(8,128)(2,1)}) custom-call(bf16[3,256,1024]{2,1,0:T(8,128)(2,1)} %bitcast.10, f32[3,7,1024]{2,1,0:T(8,128)} %bitcast.17, f32[128,1024]{1,0:T(8,128)} %bitcast.13, bf16[3,256,1024]{2,1,0:T(8,128)(2,1)} %bitcast.11, bf16[3,256,1024]{2,1,0:T(8,128)(2,1)} %bitcast.12, ...), custom_call_target="tpu_custom_call" | custom-call | tf_op jit(solution)/shard_map/pallas_call | solution.py:606
  208.7 1.9 copy.17
  210.5 1.9 copy.18

commit v3 on v2

--- a/solution.py
+++ b/solution.py
@@ -50,7 +50,7 @@
     w_ref, short_ref, long_ref, u1_ref, u2_ref, g1_ref, gl_ref, fwd_ref, inv_ref, fwd32_ref,
     out1_ref, out2_ref,
     wb, ue, ge, p0, p1, p2, mx, di, pb, rb, tb, sb, resp, pr, dm, df,
-    ring_s, ring_r, x_s, x_r, loc, halo_s, halo_r, pass_s, tp_s, tp_r, sum_s, sum_r, hop_r, main_s, main_r,
+    ring_s, ring_r, x_s, x_r, loc, halo_s, halo_r, pass_s, tp_s, tp_r, sum_s, sum_r, late_s, late_r, hop_r, main_s, main_r,
     edge_s, edge_r, fin_s, fin_r,
 ):
     s = lax.axis_index("section")
@@ -372,10 +372,22 @@
             for half in range(2):
                 half_copy(j, half).wait_send()
 
+    def sum_parts(j, q, src, to):
+        return (
+            remote(pb.at[j, other_g], rb.at[1, src, q, other_g], sum_s.at[j], sum_r.at[src, q], {"tp": to}),
+            remote(pb.at[j, own_g], rb.at[1, src, q, own_g], late_s.at[q], late_r.at[q], {"tp": to}),
+        )
+
     def end_second(j):
         kt, q = place(j)
-
-        @pl.when(kt != k)
+        in_parts = kt == (k + 1 + 2 * q) % 4
+
+        @pl.when(in_parts)
+        def _():
+            for copy in sum_parts(j, q, k, kt):
+                copy.wait_send()
+
+        @pl.when((kt != k) & jnp.logical_not(in_parts))
         def _():
             remote(pb.at[j], rb.at[1, k, q], sum_s.at[j], sum_r.at[k, q], {"tp": kt}).wait_send()
 
@@ -437,7 +449,12 @@
                 remote(pb.at[j], tb.at[q], sum_s.at[j], hop_r.at[q], {"tp": target}).wait_recv()
                 pb[j] = (pb[j].astype(f32) + tb[q].astype(f32)).astype(bf16)
 
-            @pl.when((pair == 1) | (pair == 3))
+            @pl.when(pair == 3)
+            def _():
+                for copy in sum_parts(j, q, k, target):
+                    copy.start()
+
+            @pl.when(pair == 1)
             def _():
                 remote(pb.at[j], rb.at[1, k, q], sum_s.at[j], sum_r.at[k, q], {"tp": target}).start()
 
@@ -445,13 +462,16 @@
 
         lax.fori_loop(0, 8, unit, 0)
 
-    def combine(i, q):
+    def combine(i, q, rows=None):
         cols = columns(h + 2 * q)
         steps = (1, 2, 3) if i == 0 else (1, 3)
         for step in steps:
             src = (k + step) % 4
             if i == 1:
-                remote(pb.at[0], rb.at[1, src, q], sum_s.at[0], sum_r.at[src, q], {"tp": src}).wait_recv()
+                if step == 3 - 2 * q:
+                    sum_parts(0, q, src, src)[rows].wait_recv()
+                elif rows == 0:
+                    remote(pb.at[0], rb.at[1, src, q], sum_s.at[0], sum_r.at[src, q], {"tp": src}).wait_recv()
                 continue
             for half in range(2):
                 part = pl.ds(128 * half, 128)
@@ -459,15 +479,17 @@
                        tp_r.at[src, q, half], {"tp": src}).wait_recv()
         mine = (z + 8 - 2 * k - q) % 8
 
+        start = 0 if i == 0 else 256 * ((1 - h) if rows == 0 else h)
+
         def tile(b, _):
-            here = pl.ds(pl.multiple_of(b * 64, 64), 64)
+            here = pl.ds(pl.multiple_of(start + b * 64, 64), 64)
             total = ge[i, here, cols].astype(f32) + pb[mine, here].astype(f32)
             for step in steps:
                 total += rb[i, (k + step) % 4, q, here].astype(f32)
             sb[i, q, here] = total.astype(bf16)
             return 0
 
-        lax.fori_loop(0, GROUP // 64, tile, 0)
+        lax.fori_loop(0, (GROUP if i == 0 else 256) // 64, tile, 0)
 
     outs = (out1_ref, out2_ref)
 
@@ -554,10 +576,11 @@
         give.start()
     multiply_second()
     for q in range(2):
-        combine(1, q)
-        keep, give, _ = finals(1, q)
-        give.start()
-        keep.start()
+        combine(1, q, 0)
+        finals(1, q)[1].start()
+    for q in range(2):
+        combine(1, q, 1)
+        finals(1, q)[0].start()
 
     def sent(hh):
         for to_right in (True, False):
@@ -626,7 +649,7 @@
             pltpu.VMEM((REACH, CHUNK), bf16),
             pltpu.VMEM((3, KEPT, CHUNK), f32),
             dma((2, 4, 2)), dma((2, 4, 2)), dma((4,)), dma((4,)), dma((9,)),
-            dma((2, 5)), dma((2, 5)), dma((2, 5)), dma((8, 2)), dma((4, 2, 2)), dma((8,)), dma((4, 2)), dma((2,)),
+            dma((2, 5)), dma((2, 5)), dma((2, 5)), dma((8, 2)), dma((4, 2, 2)), dma((8,)), dma((4, 2)), dma((2,)), dma((2,)), dma((2,)),
             dma((2, 2)), dma((4,)), dma((2, 2)), dma((4,)), dma((2, 2)), dma((2, 2)),
         ],
         compiler_params=pltpu.CompilerParams(

time: 215 us -> 212 us (0.986)
  no operation moved by 1% of the time
where the time goes in v3:
time: 212 us; the launch traced here: 211 us
  Pallas kernels  205 us (97%)
  local copies, waits for them, and re-layouts  5.29 us (2%)
    pallas_call x1, Pallas kernels, body(): pl.pallas_call(kernel, out_shape=(jax.ShapeDtypeStruct((256, 1024), bf16)...  205 us
    unnamed x3, local copies, waits for them, and re-layouts  5.29 us

profile of v3, /device:TPU:1, one launch (start us, length us, event | category | flops | bytes accessed | tf_op | source)
XLA Modules:
  0.0 211.1 jit_solution(16012729384951722709)
XLA Ops:
  0.6 1.6 copy.14
  2.2 205.1 %shard_map.113 = (bf16[256,1024]{1,0:T(8,128)(2,1)}, bf16[256,1024]{1,0:T(8,128)(2,1)}) custom-call(bf16[3,256,1024]{2,1,0:T(8,128)(2,1)} %bitcast.10, f32[3,7,1024]{2,1,0:T(8,128)} %bitcast.17, f32[128,1024]{1,0:T(8,128)} %bitcast.13, bf16[3,256,1024]{2,1,0:T(8,128)(2,1)} %bitcast.11, bf16[3,256,1024]{2,1,0:T(8,128)(2,1)} %bitcast.12, ...), custom_call_target="tpu_custom_call" | custom-call | tf_op jit(solution)/shard_map/pallas_call | solution.py:629
  207.3 1.9 copy.17
  209.2 1.9 copy.18
